TPU v7x, 32 devices: a whole 2x2x4 slice. The times are simulated.
32 devices in a mesh: doc: 8 (over z, y), head: 4 (over x, core).
Axes of the slice: x: 2, y: 2, z: 4, core: 2. Of those that a mesh axis runs over, the one named last changes fastest.
Arguments:
- target_q: bfloat16 [1024, 2048], P('doc', 'head'), may hold values from -300 to 300
- target_kv: bfloat16 [1024, 512], P('doc', 'head'), may hold values from -8 to 8
- doc_kv: bfloat16 [8, 384, 512], P('doc', None, 'head'), may hold values from -6 to 6
- doc_lengths: int32 [8], replicated, may hold values from 1 to 384, 2304 in all
- segment_ids: int32 [1024], replicated, may hold values from 0 to 15, never falling along the last dimension, each value on 1 to 128 neighbouring positions
- out_weight: bfloat16 [2048, 8192], P('head', 'doc'), may hold values from -0.125 to 0.125
Outputs:
- projected: bfloat16 [1024, 8192], P('head', 'doc')
Inputs may be any that keep to these rules, and one draw needn't show every extreme that they name: `segment_ids`: segment numbers never fall along the target rows, and each segment spans at most 128 rows.
All inputs are finite; a program needn't handle non-finite values.
Results may differ from a plain program's by a relative error of at most 0.005.
Values may be sent and summed in bfloat16 or wider, within the bound.
A program may use at most 64 MiB of HBM per device.

v0:
```python
import math
import jax
import jax.numpy as jnp
from jax import lax
from jax.sharding import PartitionSpec as P

masked_score = -1e30


def swapped(array, axis, stride):
    return lax.ppermute(array, axis, [(i, i ^ 1 << stride) for i in range(lax.axis_size(axis))])


def passed_along(value, axis, steps):
    count = lax.axis_size(axis)
    initial, last = (max(0, -steps), min(count, count - steps))
    return lax.ppermute(value, axis, [(source, source + steps) for source in range(initial, last)])


def block_stats(queries, key_block, value_block, visible):
    scaling = 1.0 / math.sqrt(key_block.shape[1])
    scores = (
        lax.dot_general(
            queries, key_block, (((1,), (1,)), ((), ())), preferred_element_type=jnp.float32
        )
        * scaling
    )
    scores = jnp.where(visible, scores, masked_score)
    highest = jnp.max(scores, axis=1)
    weights = jnp.exp(scores - highest[:, None])
    summed = jnp.sum(weights, axis=1)
    blended = jnp.dot(weights.astype(jnp.bfloat16), value_block, preferred_element_type=jnp.float32)
    return (highest, summed, blended)


def merge_stats(state_now, incoming):
    highest = jnp.maximum(state_now[0], incoming[0])
    old_factor = jnp.exp(state_now[0] - highest)
    new_factor = jnp.exp(incoming[0] - highest)
    summed = state_now[1] * old_factor + incoming[1] * new_factor
    blended = state_now[2] * old_factor[:, None] + incoming[2] * new_factor[:, None]
    return (highest, summed, blended)


def body(target_q, target_kv, doc_kv, doc_lengths, segment_ids, out_weight):
    row_count = target_q.shape[0]
    head_dim = target_kv.shape[1]
    per_device = target_q.shape[1] // head_dim
    queries = target_q.reshape(row_count * per_device, head_dim)
    parity = lax.axis_index("head") % 2
    doc_index = lax.axis_index("doc")

    def arrange(own_part, partner):
        return (
            jnp.where(parity == 0, own_part, partner),
            jnp.where(parity == 0, partner, own_part),
        )

    initial = (
        jnp.full((queries.shape[0],), masked_score, jnp.float32),
        jnp.zeros((queries.shape[0],), jnp.float32),
        jnp.zeros((queries.shape[0], head_dim), jnp.float32),
    )
    partner_doc, partner_tgt = swapped((doc_kv, target_kv), "head", 0)
    doc_keys, doc_values = arrange(doc_kv, partner_doc)
    key_docs = lax.all_gather(doc_keys, "doc", axis=0, tiled=True)
    value_docs = lax.all_gather(doc_values, "doc", axis=0, tiled=True)
    slot_index = jnp.arange(key_docs.shape[1], dtype=jnp.int32)

    def attend_doc(doc_step, running):
        key_block = lax.dynamic_index_in_dim(key_docs, doc_step, 0, keepdims=False)
        value_block = lax.dynamic_index_in_dim(value_docs, doc_step, 0, keepdims=False)
        length = lax.dynamic_index_in_dim(doc_lengths, doc_step, 0, keepdims=False)
        visible = (slot_index < length)[None, :]
        return merge_stats(running, block_stats(queries, key_block, value_block, visible))

    stats = lax.fori_loop(0, key_docs.shape[0], attend_doc, initial)
    own_keys, own_values = arrange(target_kv, partner_tgt)
    prev_keys, prev_values = passed_along((own_keys, own_values), "doc", 1)
    own_seg = lax.dynamic_slice_in_dim(segment_ids, doc_index * row_count, row_count)
    prev_start = jnp.maximum(doc_index - 1, 0) * row_count
    prev_seg = jnp.where(
        doc_index > 0, lax.dynamic_slice_in_dim(segment_ids, prev_start, row_count), -1
    )
    token_pos = jnp.arange(row_count, dtype=jnp.int32)
    own_mask = (own_seg[:, None] == own_seg[None, :]) & (token_pos[None, :] <= token_pos[:, None])
    prev_mask = own_seg[:, None] == prev_seg[None, :]
    stats = merge_stats(
        stats, block_stats(queries, own_keys, own_values, jnp.repeat(own_mask, per_device, axis=0))
    )
    stats = merge_stats(
        stats,
        block_stats(queries, prev_keys, prev_values, jnp.repeat(prev_mask, per_device, axis=0)),
    )
    attention = (
        (stats[2] / stats[1][:, None])
        .astype(jnp.bfloat16)
        .reshape(row_count, per_device * head_dim)
    )
    gathered = lax.all_gather(attention, "doc", axis=0, tiled=True)
    result = lax.psum_scatter(
        jnp.dot(gathered, out_weight, preferred_element_type=jnp.float32),
        "head",
        scatter_dimension=0,
        tiled=True,
    )
    return result.astype(jnp.bfloat16)


def solution(mesh):
    placed = (
        P("doc", "head"),
        P("doc", "head"),
        P("doc", None, "head"),
        P(),
        P(),
        P("head", "doc"),
    )
    return jax.shard_map(
        body, mesh=mesh, in_specs=placed, out_specs=P("head", "doc"), check_vma=False
    )
```

profile of v0, /device:TPU:0, one launch (start us, length us, event | category | flops | bytes accessed | tf_op | source)
XLA Modules:
  0.0 207.3 jit_solution(15352952914273228183)
XLA Ops:
  6.5 0.5 collective-permute-start.1
  7.1 0.8 fusion.38
  8.1 0.1 copy.9
  8.3 0.1 copy.10
  8.5 1.0 reshape.30
  9.5 1.4 broadcast_select_fusion.3
  10.9 4.9 %collective-permute-start.2 = (bf16[128,128]{1,0:T(8,128)(2,1)S(1)}, bf16[128,128]{1,0:T(8,128)(2,1)S(1)}, u32[]{:S(2)}, u32[]{:S(2)}) collective-permute-start(bf16[128,128]{1,0:T(8,128)(2,1)S(1)} %get-tuple-element.222), channel_id=1, source_target_pairs={{0,4},{4,8},{8,12},{12,16},{16,20},{20,24},{24,28},{1,5},{5,9},{9,... | collective-permute-start | bytes 98312 | tf_op jit(solution)/shard_map/ppermute | solution.py:17
  15.7 4.0 %collective-permute-start.3 = (bf16[128,128]{1,0:T(8,128)(2,1)}, bf16[128,128]{1,0:T(8,128)(2,1)}, u32[]{:S(2)}, u32[]{:S(2)}) collective-permute-start(bf16[128,128]{1,0:T(8,128)(2,1)} %get-tuple-element.223), channel_id=1, source_target_pairs={{0,4},{4,8},{8,12},{12,16},{16,20},{20,24},{24,28},{1,5},{5,9},{9,... | collective-permute-start | bytes 98312 | tf_op jit(solution)/shard_map/ppermute | solution.py:17
  19.8 0.2 fusion.40
  20.0 0.6 fusion.24
  20.6 0.2 fusion.39
  20.8 0.6 fusion.26
  21.5 0.9 broadcast_select_fusion
  22.4 32.1 %all_gather.10 = bf16[8,384,128]{2,1,0:T(8,128)(2,1)S(1)} all-gather(bf16[1,384,128]{2,1,0:T(8,128)(2,1)S(1)} %get-tuple-element.220), channel_id=1, replica_groups=mesh['doc'=8,'head'=4] {'doc'}, dimensions={0}, use_global_device_ids=true | all-gather | bytes 884736 | tf_op jit(solution)/shard_map/all_gather | solution.py:67
  54.5 32.1 %all_gather.9 = bf16[8,384,128]{2,1,0:T(8,128)(2,1)S(1)} all-gather(bf16[1,384,128]{2,1,0:T(8,128)(2,1)S(1)} %get-tuple-element.221), channel_id=1, replica_groups=mesh['doc'=8,'head'=4] {'doc'}, dimensions={0}, use_global_device_ids=true | all-gather | bytes 884736 | tf_op jit(solution)/shard_map/all_gather | solution.py:66
  86.7 21.7 %while.18 = (s32[]{:T(128)}, f32[512]{0:T(512)S(1)}, f32[512]{0:T(512)S(1)}, f32[512,128]{1,0:T(8,128)S(1)}, s32[8]{0:T(128)}, /*index=5*/bf16[8,384,128]{2,1,0:...) while((s32[]{:T(128)}, f32[512]{0:T(512)S(1)}, ...), condition=%wide.region_3.4_spmd.clone, body=%wide.region_0.3_spmd.clone.sunk | while | flops 102305152 | bytes 3240976 | solution.py:77
  86.7 1.2 dynamic_slice.51
  87.9 0.6 iota_compare_fusion.3
  88.5 0.3 fusion.61
  88.8 0.2 fusion.62
  88.9 0.4 fusion.64
  89.4 1.2 dynamic_slice.51
  90.6 0.6 iota_compare_fusion.3
  91.2 0.3 fusion.61
  91.5 0.2 fusion.62
  91.6 0.4 fusion.64
  92.1 1.2 dynamic_slice.51
  93.3 0.6 iota_compare_fusion.3
  93.9 0.3 fusion.61
  94.2 0.2 fusion.62
  94.3 0.4 fusion.64
  94.8 1.2 dynamic_slice.51
  96.0 0.6 iota_compare_fusion.3
  96.6 0.3 fusion.61
  96.9 0.2 fusion.62
  97.1 0.4 fusion.64
  97.5 1.2 dynamic_slice.51
  98.7 0.6 iota_compare_fusion.3
  99.3 0.3 fusion.61
  99.6 0.2 fusion.62
  99.8 0.4 fusion.64
  100.2 1.2 dynamic_slice.51
  101.4 0.6 iota_compare_fusion.3
  102.0 0.3 fusion.61
  102.3 0.2 fusion.62
  102.5 0.4 fusion.64
  102.9 1.2 dynamic_slice.51
  104.2 0.6 iota_compare_fusion.3
  104.7 0.3 fusion.61
  105.0 0.2 fusion.62
  105.2 0.4 fusion.64
  105.6 1.2 dynamic_slice.51
  106.9 0.6 iota_compare_fusion.3
  107.4 0.3 fusion.61
  107.7 0.2 fusion.62
  107.9 0.4 fusion.64
  108.3 0.7 multiply_add_fusion
  109.0 1.0 convolution_multiply_fusion.2
  110.0 1.2 fusion.23
  111.2 0.7 reshape.33
  112.0 38.6 %all-gather.2.cloned.1.call-done = bf16[1024,512]{1,0:T(8,128)(2,1)} async-done(((bf16[128,512]{1,0:T(8,128)(2,1)}), bf16[1024,512]{1,0:T(8,128)(2,1)}) %all-gather.2.cloned.1.call-update) | async-done | bytes 1048592 | tf_op jit(solution)/shard_map/all_gather | solution.py:100
  150.6 4.4 %fusion.41 = f32[1024,1024]{1,0:T(8,128)} fusion(bf16[1024,512]{1,0:T(8,128)(2,1)} %all-gather.2.cloned.1.call-done, bf16[512,1024]{1,0:T(8,128)(2,1)S(1)} %copy-done), kind=kOutput, calls=%fused_computation.62 | convolution fusion | flops 1073741824 | bytes 6291456 | tf_op jit(solution)/shard_map/dot_general | solution.py:102
  155.0 43.4 %reduce-scatter.2.cloned.1.call-done = f32[256,1024]{1,0:T(8,128)} async-done(((f32[1024,1024]{1,0:T(8,128)}), f32[256,1024]{1,0:T(8,128)}) %reduce-scatter.2.cloned.1.call-update) | async-done | bytes 1048592 | tf_op jit(solution)/shard_map/reduce_scatter | solution.py:101
  198.4 2.1 %convert_element_type.20 = bf16[256,1024]{1,0:T(8,128)(2,1)} convert(f32[256,1024]{1,0:T(8,128)} %reduce-scatter.2.cloned.1.call-done) | non-fusion elementwise | flops 262144 | bytes 1572864 | tf_op jit(solution)/shard_map/convert_element_type | solution.py:107
  (25 shorter events, 0.5 us)
Async XLA Ops:
  6.5 144.0 %copy-start = (bf16[512,1024]{1,0:T(8,128)(2,1)S(1)}, bf16[512,1024]{1,0:T(8,128)(2,1)}, u32[]{:S(2)}) copy-start(bf16[512,1024]{1,0:T(8,128)(2,1)} %param.13) | copy-start | bytes 3145732
  6.5 144.0 %all-gather.2.cloned.1.call-start = ((), (), s32[]{:S(2)}) async-start(), calls=%async_computation.1 | async-start | bytes 1179648 | tf_op jit(solution)/shard_map/all_gather | solution.py:100
  6.5 2.9 %collective-permute-start.1 = (bf16[128,128]{1,0:T(8,128)(2,1)}, bf16[128,128]{1,0:T(8,128)(2,1)S(1)}, u32[]{:S(2)}, u32[]{:S(2)}) collective-permute-start(bf16[128,128]{1,0:T(8,128)(2,1)} %param.9), channel_id=1, source_target_pairs={{0,1},{1,0},{2,3},{3,2},{4,5},{5,4},{6,7},{7,6},{8,9},{9,8},{10,11... | collective-permute-start | bytes 98312 | tf_op jit(solution)/shard_map/ppermute | solution.py:11
  7.0 14.5 %collective-permute-start = (bf16[1,384,128]{2,1,0:T(8,128)(2,1)}, bf16[1,384,128]{2,1,0:T(8,128)(2,1)S(1)}, u32[]{:S(2)}, u32[]{:S(2)}) collective-permute-start(bf16[1,384,128]{2,1,0:T(8,128)(2,1)} %param.10), channel_id=1, source_target_pairs={{0,1},{1,0},{2,3},{3,2},{4,5},{5,4},{6,7},{7,6},{8,9},{9,8},{10,11... | collective-permute-start | bytes 294920 | tf_op jit(solution)/shard_map/ppermute | solution.py:11
  10.9 9.8 %collective-permute-start.2 = (bf16[128,128]{1,0:T(8,128)(2,1)S(1)}, bf16[128,128]{1,0:T(8,128)(2,1)S(1)}, u32[]{:S(2)}, u32[]{:S(2)}) collective-permute-start(bf16[128,128]{1,0:T(8,128)(2,1)S(1)} %get-tuple-element.222), channel_id=1, source_target_pairs={{0,4},{4,8},{8,12},{12,16},{16,20},{20,24},{24,28},{1,5},{5,9},{9,... | collective-permute-start | bytes 98312 | tf_op jit(solution)/shard_map/ppermute | solution.py:17
  15.7 93.3 %collective-permute-start.3 = (bf16[128,128]{1,0:T(8,128)(2,1)}, bf16[128,128]{1,0:T(8,128)(2,1)}, u32[]{:S(2)}, u32[]{:S(2)}) collective-permute-start(bf16[128,128]{1,0:T(8,128)(2,1)} %get-tuple-element.223), channel_id=1, source_target_pairs={{0,4},{4,8},{8,12},{12,16},{16,20},{20,24},{24,28},{1,5},{5,9},{9,... | collective-permute-start | bytes 98312 | tf_op jit(solution)/shard_map/ppermute | solution.py:17
  111.9 86.5 %reduce-scatter.2.cloned.1.call-start = ((), (), s32[]{:S(2)}) async-start(), calls=%async_computation.2 | async-start | bytes 5242880 | tf_op jit(solution)/shard_map/reduce_scatter | solution.py:101
Sparse Core Ops, SparseCore 0:
  112.1 38.4 all-gather.1
  155.1 43.2 reduce-scatter.1
where the time goes:
time: 208 us; the launch traced here: 207 us
  waiting for transfers between devices  82 us (39%)
  blocking collectives  64.3 us (31%)
  between operations  13.6 us (7%)
  other arithmetic  13.1 us (6%)
  matrix products  12.6 us (6%)
  local copies, waits for them, and re-layouts  12 us (6%)
  starting transfers between devices  9.46 us (5%)
    reduce_scatter x1, waiting for transfers between devices, body(): lax.psum_scatter(jnp.dot(gathered, out_weight, preferred_element_type=jnp...  43.4 us
    all_gather x1, waiting for transfers between devices, body(): gathered = lax.all_gather(attention, 'doc', axis=0, tiled=True)  38.6 us
    all_gather x1, blocking collectives, body(): key_docs = lax.all_gather(doc_keys, 'doc', axis=0, tiled=True)  32.1 us
    all_gather x1, blocking collectives, body(): value_docs = lax.all_gather(doc_values, 'doc', axis=0, tiled=True)  32.1 us
    dynamic_slice x8, local copies, waits for them, and re-layouts, attend_doc(): length = lax.dynamic_index_in_dim(doc_lengths, doc_step, 0, keepdims=False)  9.87 us
    ppermute x2, starting transfers between devices, passed_along(): lax.ppermute(value, axis, [(source, source + steps) for source in range(i...  8.91 us
    dot_general x10, matrix products, block_stats(): jnp.dot(weights.astype(jnp.bfloat16), value_block, preferred_element_type...  5.52 us
    lt x8, other arithmetic, attend_doc(): visible = (slot_index < length)[None, :]  4.5 us
  transfers between devices with their start and end apart: 6, of which 2 were waited for; matrix products, arithmetic and copies ran while one was open for 14% of the time, Pallas kernels for 0%

commit v1 on v0

--- a/solution.py
+++ b/solution.py
@@ -64,7 +64,12 @@
     partner_doc, partner_tgt = swapped((doc_kv, target_kv), "head", 0)
     doc_keys, doc_values = arrange(doc_kv, partner_doc)
     key_docs = lax.all_gather(doc_keys, "doc", axis=0, tiled=True)
-    value_docs = lax.all_gather(doc_values, "doc", axis=0, tiled=True)
+    ring = [doc_values]
+    for hop in range(7):
+        ring.append(lax.ppermute(ring[-1], "doc", [(dev, (dev + 1) % 8) for dev in range(8)]))
+    value_docs = jnp.roll(
+        jnp.concatenate(ring[::-1], axis=0), (lax.axis_index("doc") + 1) * ring[0].shape[0], axis=0
+    )
     slot_index = jnp.arange(key_docs.shape[1], dtype=jnp.int32)
 
     def attend_doc(doc_step, running):

time: 208 us -> 221 us (1.062)
  waiting for transfers between devices: 82 us -> 116 us
  blocking collectives: 64.3 us -> 32.8 us
  matrix products: 12.6 us -> 19.8 us
    all_gather x1 -> x0, blocking collectives: 32.1 us -> none  [body(): value_docs = lax.all_gather(doc_values, 'doc', axis=0, tiled=True)]
    ppermute x0 -> x7, waiting for transfers between devices: none -> 31 us  [body(): lax.ppermute(ring[-1], 'doc', [(dev, (dev + 1) % 8) for dev in range(8)])]
    dot_general x10, matrix products: 5.52 us -> 12.7 us  [block_stats(): jnp.dot(weights.astype(jnp.bfloat16), value_block, preferred_element_type...]
    ppermute x0 -> x7, starting transfers between devices: none -> 4.83 us  [body(): lax.ppermute(ring[-1], 'doc', [(dev, (dev + 1) % 8) for dev in range(8)])]
    ppermute x2, starting transfers between devices: 8.91 us -> 6.14 us  [passed_along(): lax.ppermute(value, axis, [(source, source + steps) for source in range(i...]
    all_gather x1, waiting for transfers between devices: 38.6 us -> 41.1 us  [body(): gathered = lax.all_gather(attention, 'doc', axis=0, tiled=True)]
  transfers between devices with their start and end apart: 6 -> 13, of which waited for: 2 -> 8; matrix products, arithmetic and copies ran while one was open for 14% -> 17% of each run, Pallas kernels for 0% -> 0%
where the time goes in v1:
time: 221 us; the launch traced here: 220 us
  waiting for transfers between devices  116 us (52%)
  blocking collectives  32.8 us (15%)
  matrix products  19.8 us (9%)
  between operations  13.7 us (6%)
  local copies, waits for them, and re-layouts  13.3 us (6%)
  other arithmetic  13.2 us (6%)
  starting transfers between devices  11.5 us (5%)
    reduce_scatter x1, waiting for transfers between devices, body(): lax.psum_scatter(jnp.dot(gathered, out_weight, preferred_element_type=jnp...  43.4 us
    all_gather x1, waiting for transfers between devices, body(): gathered = lax.all_gather(attention, 'doc', axis=0, tiled=True)  41.1 us
    all_gather x1, blocking collectives, body(): key_docs = lax.all_gather(doc_keys, 'doc', axis=0, tiled=True)  32.8 us
    ppermute x7, waiting for transfers between devices, body(): lax.ppermute(ring[-1], 'doc', [(dev, (dev + 1) % 8) for dev in range(8)])  31 us
    dot_general x10, matrix products, block_stats(): jnp.dot(weights.astype(jnp.bfloat16), value_block, preferred_element_type...  12.7 us
    dynamic_slice x8, local copies, waits for them, and re-layouts, attend_doc(): length = lax.dynamic_index_in_dim(doc_lengths, doc_step, 0, keepdims=False)  9.93 us
    ppermute x2, starting transfers between devices, passed_along(): lax.ppermute(value, axis, [(source, source + steps) for source in range(i...  6.14 us
    ppermute x7, starting transfers between devices, body(): lax.ppermute(ring[-1], 'doc', [(dev, (dev + 1) % 8) for dev in range(8)])  4.83 us
  transfers between devices with their start and end apart: 13, of which 8 were waited for; matrix products, arithmetic and copies ran while one was open for 17% of the time, Pallas kernels for 0%

profile of v1, /device:TPU:0, one launch (start us, length us, event | category | flops | bytes accessed | tf_op | source)
XLA Modules:
  0.0 220.3 jit_solution(2083544164685528893)
XLA Ops:
  6.5 0.5 collective-permute-start
  7.1 0.8 fusion.38
  7.9 0.3 collective-permute-done
  8.1 0.9 broadcast_select_fusion
  9.1 2.9 %collective-permute-start.1 = (bf16[1,384,128]{2,1,0:T(8,128)(2,1)S(1)}, bf16[1,384,128]{2,1,0:T(8,128)(2,1)S(1)}, u32[]{:S(2)}, u32[]{:S(2)}) collective-permute-start(bf16[1,384,128]{2,1,0:T(8,128)(2,1)S(1)} %get-tuple-element.220), channel_id=1, source_target_pairs={{0,4},{4,8},{8,12},{12,16},{16,20},{20,24},{24,28},{28,0},{1,5},{5... | collective-permute-start | bytes 294920 | tf_op jit(solution)/shard_map/ppermute | solution.py:69
  12.1 1.0 reshape.30
  13.6 4.6 %collective-permute-done.1 = bf16[1,384,128]{2,1,0:T(8,128)(2,1)S(1)} collective-permute-done((bf16[1,384,128]{2,1,0:T(8,128)(2,1)S(1)}, bf16[1,384,128]{2,1,0:T(8,128)(2,1)S(1)}, u32[]{:S(2)}, u32[]{:S(2)}) %collective-permute-start.1) | collective-permute-done | bytes 98336 | tf_op jit(solution)/shard_map/ppermute | solution.py:69
  18.1 1.4 broadcast_select_fusion.3
  19.5 3.0 %collective-permute-start.9 = (bf16[128,128]{1,0:T(8,128)(2,1)S(1)}, bf16[128,128]{1,0:T(8,128)(2,1)S(1)}, u32[]{:S(2)}, u32[]{:S(2)}) collective-permute-start(bf16[128,128]{1,0:T(8,128)(2,1)S(1)} %get-tuple-element.222), channel_id=1, source_target_pairs={{0,4},{4,8},{8,12},{12,16},{16,20},{20,24},{24,28},{1,5},{5,9},{9,... | collective-permute-start | bytes 98312 | tf_op jit(solution)/shard_map/ppermute | solution.py:17
  22.5 3.1 %collective-permute-start.10 = (bf16[128,128]{1,0:T(8,128)(2,1)}, bf16[128,128]{1,0:T(8,128)(2,1)}, u32[]{:S(2)}, u32[]{:S(2)}) collective-permute-start(bf16[128,128]{1,0:T(8,128)(2,1)} %get-tuple-element.223), channel_id=1, source_target_pairs={{0,4},{4,8},{8,12},{12,16},{16,20},{20,24},{24,28},{1,5},{5,9},{9,... | collective-permute-start | bytes 98312 | tf_op jit(solution)/shard_map/ppermute | solution.py:17
  25.7 1.9 collective-permute-start.3
  27.6 0.2 fusion.40
  27.8 5.2 %collective-permute-done.3 = bf16[1,384,128]{2,1,0:T(8,128)(2,1)S(1)} collective-permute-done((bf16[1,384,128]{2,1,0:T(8,128)(2,1)S(1)}, bf16[1,384,128]{2,1,0:T(8,128)(2,1)S(1)}, u32[]{:S(2)}, u32[]{:S(2)}) %collective-permute-start.3) | collective-permute-done | bytes 98336 | tf_op jit(solution)/shard_map/ppermute | solution.py:69
  33.0 0.6 fusion.24
  33.6 6.7 %collective-permute-done.4 = bf16[1,384,128]{2,1,0:T(8,128)(2,1)S(1)} collective-permute-done((bf16[1,384,128]{2,1,0:T(8,128)(2,1)S(1)}, bf16[1,384,128]{2,1,0:T(8,128)(2,1)S(1)}, u32[]{:S(2)}, u32[]{:S(2)}) %collective-permute-start.4) | collective-permute-done | bytes 98336 | tf_op jit(solution)/shard_map/ppermute | solution.py:69
  40.3 0.2 fusion.39
  40.5 7.1 %collective-permute-done.5 = bf16[1,384,128]{2,1,0:T(8,128)(2,1)S(1)} collective-permute-done((bf16[1,384,128]{2,1,0:T(8,128)(2,1)S(1)}, bf16[1,384,128]{2,1,0:T(8,128)(2,1)S(1)}, u32[]{:S(2)}, u32[]{:S(2)}) %collective-permute-start.5) | collective-permute-done | bytes 98336 | tf_op jit(solution)/shard_map/ppermute | solution.py:69
  47.6 0.7 fusion.26
  48.3 7.5 %collective-permute-done.6 = bf16[1,384,128]{2,1,0:T(8,128)(2,1)S(1)} collective-permute-done((bf16[1,384,128]{2,1,0:T(8,128)(2,1)S(1)}, bf16[1,384,128]{2,1,0:T(8,128)(2,1)S(1)}, u32[]{:S(2)}, u32[]{:S(2)}) %collective-permute-start.6) | collective-permute-done | bytes 98336 | tf_op jit(solution)/shard_map/ppermute | solution.py:69
  55.8 32.8 %all_gather.6 = bf16[8,384,128]{2,1,0:T(8,128)(2,1)S(1)} all-gather(bf16[1,384,128]{2,1,0:T(8,128)(2,1)S(1)} %get-tuple-element.221), channel_id=1, replica_groups=mesh['doc'=8,'head'=4] {'doc'}, dimensions={0}, use_global_device_ids=true | all-gather | bytes 884736 | tf_op jit(solution)/shard_map/all_gather | solution.py:66
  88.9 0.9 constant_dynamic-slice_fusion
  89.9 28.8 %while.18 = (s32[]{:T(128)}, f32[512]{0:T(512)S(1)}, f32[512]{0:T(512)S(1)}, f32[512,128]{1,0:T(8,128)S(1)}, s32[8]{0:T(128)}, /*index=5*/bf16[8,384,128]{2,1,0:...) while((s32[]{:T(128)}, f32[512]{0:T(512)S(1)}, ...), condition=%wide.region_3.4_spmd.clone, body=%wide.region_0.3_spmd.clone.sunk | while | flops 102305152 | bytes 3241476 | solution.py:82
  89.9 1.2 dynamic_slice.57
  91.1 0.6 iota_compare_fusion.3
  91.7 0.3 fusion.61
  92.1 1.3 fusion.64
  93.5 1.2 dynamic_slice.57
  94.7 0.6 iota_compare_fusion.3
  95.3 0.3 fusion.61
  95.7 1.3 fusion.64
  97.1 1.2 dynamic_slice.57
  98.3 0.6 iota_compare_fusion.3
  98.9 0.3 fusion.61
  99.3 1.3 fusion.64
  100.7 1.2 dynamic_slice.57
  101.9 0.6 iota_compare_fusion.3
  102.5 0.3 fusion.61
  102.9 1.3 fusion.64
  104.3 1.2 dynamic_slice.57
  105.5 0.6 iota_compare_fusion.3
  106.1 0.3 fusion.61
  106.6 1.3 fusion.64
  107.9 1.2 dynamic_slice.57
  109.1 0.6 iota_compare_fusion.3
  109.7 0.3 fusion.61
  110.0 0.2 fusion.62
  110.2 1.3 fusion.64
  111.5 1.2 dynamic_slice.57
  112.7 0.6 iota_compare_fusion.3
  113.3 0.3 fusion.61
  113.6 0.2 fusion.62
  113.8 1.3 fusion.64
  115.1 1.2 dynamic_slice.57
  116.3 0.6 iota_compare_fusion.3
  116.9 0.3 fusion.61
  117.4 1.3 fusion.64
  118.7 0.7 multiply_add_fusion
  119.4 1.0 convolution_multiply_fusion.2
  120.4 1.2 fusion.23
  121.6 0.7 reshape.33
  122.4 41.1 %all-gather.2.cloned.1.call-done = bf16[1024,512]{1,0:T(8,128)(2,1)} async-done(((bf16[128,512]{1,0:T(8,128)(2,1)}), bf16[1024,512]{1,0:T(8,128)(2,1)}) %all-gather.2.cloned.1.call-update) | async-done | bytes 1048592 | tf_op jit(solution)/shard_map/all_gather | solution.py:105
  163.5 4.4 %fusion.41 = f32[1024,1024]{1,0:T(8,128)} fusion(bf16[1024,512]{1,0:T(8,128)(2,1)} %all-gather.2.cloned.1.call-done, bf16[512,1024]{1,0:T(8,128)(2,1)S(1)} %copy-done), kind=kOutput, calls=%fused_computation.79 | convolution fusion | flops 1073741824 | bytes 6291456 | tf_op jit(solution)/shard_map/dot_general | solution.py:107
  168.0 43.4 %reduce-scatter.2.cloned.1.call-done = f32[256,1024]{1,0:T(8,128)} async-done(((f32[1024,1024]{1,0:T(8,128)}), f32[256,1024]{1,0:T(8,128)}) %reduce-scatter.2.cloned.1.call-update) | async-done | bytes 1048592 | tf_op jit(solution)/shard_map/reduce_scatter | solution.py:106
  211.4 2.1 convert_element_type.20
  (59 shorter events, 2.0 us)
Async XLA Ops:
  6.5 157.0 %copy-start = (bf16[512,1024]{1,0:T(8,128)(2,1)S(1)}, bf16[512,1024]{1,0:T(8,128)(2,1)}, u32[]{:S(2)}) copy-start(bf16[512,1024]{1,0:T(8,128)(2,1)} %param.13) | copy-start | bytes 3145732
  6.5 157.0 %all-gather.2.cloned.1.call-start = ((), (), s32[]{:S(2)}) async-start(), calls=%async_computation.1 | async-start | bytes 1179648 | tf_op jit(solution)/shard_map/all_gather | solution.py:105
  6.5 1.6 collective-permute-start
  7.0 11.1 %collective-permute-start.8 = (bf16[128,128]{1,0:T(8,128)(2,1)}, bf16[128,128]{1,0:T(8,128)(2,1)S(1)}, u32[]{:S(2)}, u32[]{:S(2)}) collective-permute-start(bf16[128,128]{1,0:T(8,128)(2,1)} %param.9), channel_id=1, source_target_pairs={{0,1},{1,0},{2,3},{3,2},{4,5},{5,4},{6,7},{7,6},{8,9},{9,8},{10,11... | collective-permute-start | bytes 98312 | tf_op jit(solution)/shard_map/ppermute | solution.py:11
  9.1 9.1 %collective-permute-start.1 = (bf16[1,384,128]{2,1,0:T(8,128)(2,1)S(1)}, bf16[1,384,128]{2,1,0:T(8,128)(2,1)S(1)}, u32[]{:S(2)}, u32[]{:S(2)}) collective-permute-start(bf16[1,384,128]{2,1,0:T(8,128)(2,1)S(1)} %get-tuple-element.220), channel_id=1, source_target_pairs={{0,4},{4,8},{8,12},{12,16},{16,20},{20,24},{24,28},{28,0},{1,5},{5... | collective-permute-start | bytes 294920 | tf_op jit(solution)/shard_map/ppermute | solution.py:69
  18.1 7.5 %collective-permute-start.2 = (bf16[1,384,128]{2,1,0:T(8,128)(2,1)S(1)}, bf16[1,384,128]{2,1,0:T(8,128)(2,1)S(1)}, u32[]{:S(2)}, u32[]{:S(2)}) collective-permute-start(bf16[1,384,128]{2,1,0:T(8,128)(2,1)S(1)} %collective-permute-done.1), channel_id=1, source_target_pairs={{0,4},{4,8},{8,12},{12,16},{16,20},{20,24},{24,28},{28,0},{1,5},{5... | collective-permute-start | bytes 294920 | tf_op jit(solution)/shard_map/ppermute | solution.py:69
  19.5 20.8 %collective-permute-start.9 = (bf16[128,128]{1,0:T(8,128)(2,1)S(1)}, bf16[128,128]{1,0:T(8,128)(2,1)S(1)}, u32[]{:S(2)}, u32[]{:S(2)}) collective-permute-start(bf16[128,128]{1,0:T(8,128)(2,1)S(1)} %get-tuple-element.222), channel_id=1, source_target_pairs={{0,4},{4,8},{8,12},{12,16},{16,20},{20,24},{24,28},{1,5},{5,9},{9,... | collective-permute-start | bytes 98312 | tf_op jit(solution)/shard_map/ppermute | solution.py:17
  22.5 96.9 %collective-permute-start.10 = (bf16[128,128]{1,0:T(8,128)(2,1)}, bf16[128,128]{1,0:T(8,128)(2,1)}, u32[]{:S(2)}, u32[]{:S(2)}) collective-permute-start(bf16[128,128]{1,0:T(8,128)(2,1)} %get-tuple-element.223), channel_id=1, source_target_pairs={{0,4},{4,8},{8,12},{12,16},{16,20},{20,24},{24,28},{1,5},{5,9},{9,... | collective-permute-start | bytes 98312 | tf_op jit(solution)/shard_map/ppermute | solution.py:17
  25.7 7.3 %collective-permute-start.3 = (bf16[1,384,128]{2,1,0:T(8,128)(2,1)S(1)}, bf16[1,384,128]{2,1,0:T(8,128)(2,1)S(1)}, u32[]{:S(2)}, u32[]{:S(2)}) collective-permute-start(bf16[1,384,128]{2,1,0:T(8,128)(2,1)S(1)} %collective-permute-done.2), channel_id=1, source_target_pairs={{0,4},{4,8},{8,12},{12,16},{16,20},{20,24},{24,28},{28,0},{1,5},{5... | collective-permute-start | bytes 294920 | tf_op jit(solution)/shard_map/ppermute | solution.py:69
  27.8 12.5 %copy-start.2 = (f32[512]{0:T(512)}, f32[512]{0:T(512)S(1)}, u32[]{:S(2)}) copy-start(f32[512]{0:T(512)S(1)} %get-tuple-element.230) | copy-start | bytes 6148
  33.0 7.3 %collective-permute-start.4 = (bf16[1,384,128]{2,1,0:T(8,128)(2,1)S(1)}, bf16[1,384,128]{2,1,0:T(8,128)(2,1)S(1)}, u32[]{:S(2)}, u32[]{:S(2)}) collective-permute-start(bf16[1,384,128]{2,1,0:T(8,128)(2,1)S(1)} %collective-permute-done.3), channel_id=1, source_target_pairs={{0,4},{4,8},{8,12},{12,16},{16,20},{20,24},{24,28},{28,0},{1,5},{5... | collective-permute-start | bytes 294920 | tf_op jit(solution)/shard_map/ppermute | solution.py:69
  40.3 7.3 %collective-permute-start.5 = (bf16[1,384,128]{2,1,0:T(8,128)(2,1)S(1)}, bf16[1,384,128]{2,1,0:T(8,128)(2,1)S(1)}, u32[]{:S(2)}, u32[]{:S(2)}) collective-permute-start(bf16[1,384,128]{2,1,0:T(8,128)(2,1)S(1)} %collective-permute-done.4), channel_id=1, source_target_pairs={{0,4},{4,8},{8,12},{12,16},{16,20},{20,24},{24,28},{28,0},{1,5},{5... | collective-permute-start | bytes 294920 | tf_op jit(solution)/shard_map/ppermute | solution.py:69
  40.5 49.3 %copy-start.1 = (f32[512]{0:T(512)}, f32[512]{0:T(512)S(1)}, u32[]{:S(2)}) copy-start(f32[512]{0:T(512)S(1)} %get-tuple-element.228) | copy-start | bytes 6148
  47.6 8.1 %collective-permute-start.6 = (bf16[1,384,128]{2,1,0:T(8,128)(2,1)S(1)}, bf16[1,384,128]{2,1,0:T(8,128)(2,1)S(1)}, u32[]{:S(2)}, u32[]{:S(2)}) collective-permute-start(bf16[1,384,128]{2,1,0:T(8,128)(2,1)S(1)} %collective-permute-done.5), channel_id=1, source_target_pairs={{0,4},{4,8},{8,12},{12,16},{16,20},{20,24},{24,28},{28,0},{1,5},{5... | collective-permute-start | bytes 294920 | tf_op jit(solution)/shard_map/ppermute | solution.py:69
  55.8 32.8 %collective-permute-start.7 = (bf16[1,384,128]{2,1,0:T(8,128)(2,1)S(1)}, bf16[1,384,128]{2,1,0:T(8,128)(2,1)S(1)}, u32[]{:S(2)}, u32[]{:S(2)}) collective-permute-start(bf16[1,384,128]{2,1,0:T(8,128)(2,1)S(1)} %collective-permute-done.6), channel_id=1, source_target_pairs={{0,4},{4,8},{8,12},{12,16},{16,20},{20,24},{24,28},{28,0},{1,5},{5... | collective-permute-start | bytes 294920 | tf_op jit(solution)/shard_map/ppermute | solution.py:69
  122.4 89.0 %reduce-scatter.2.cloned.1.call-start = ((), (), s32[]{:S(2)}) async-start(), calls=%async_computation.2 | async-start | bytes 5242880 | tf_op jit(solution)/shard_map/reduce_scatter | solution.py:106
Sparse Core Ops, SparseCore 0:
  122.5 40.9 all-gather.1
  168.1 43.2 reduce-scatter.1
